TPU v7x, 32 devices: a whole 2x2x4 slice. The times are simulated.
32 devices in a mesh: parts: 2 (over x), pool: 4 (over y, core), tp: 4 (over z).
Axes of the slice: x: 2, y: 2, z: 4, core: 2. Of those that a mesh axis runs over, the one named last changes fastest.
Arguments:
- residual: bfloat16 [512, 4096], P(('parts', 'pool', 'tp')), parts along dimension 0, may hold values from -6 to 6
- queries: bfloat16 [512, 2048], P(('parts', 'pool'), 'tp'), parts along dimension 0, may hold values from -24 to 24
- new_kv: bfloat16 [2, 512, 1024], P(None, ('parts', 'pool'), 'tp'), parts along dimension 1, may hold values from -4 to 4
- cache: bfloat16 [2, 16, 512, 1024], P(None, ('parts', 'pool'), None, 'tp'), parts along dimension 1, may hold values from -20 to 20
- cache_len: int32 [16], P(('parts', 'pool')), parts along dimension 0, may hold values from 128 to 512, as said below
- draft_count: int32 [16], P(('parts', 'pool')), parts along dimension 0, may hold values from 1 to 32, as said below
- out_proj: bfloat16 [2048, 4096], P('tp'), may hold values from -0.5 to 0.5
- norm_gain: float32 [4096], replicated, may hold values from 0.1 to 1.9
- routes: int32 [512, 2], P(('parts', 'pool', 'tp')), parts along dimension 0, may hold values from 0 to 3, as said below
- slots: int32 [512, 2], P(('parts', 'pool', 'tp')), parts along dimension 0, may hold values from -1 to 11, as said below
- route_weights: bfloat16 [512, 2], P(('parts', 'pool', 'tp')), parts along dimension 0, may hold values from 0.099609375 to 1
- w_gate: bfloat16 [4, 4096, 3200], P('pool', None, 'tp'), may hold values from -0.09375 to 0.09375
- w_up: bfloat16 [4, 4096, 3200], P('pool', None, 'tp'), may hold values from -0.09375 to 0.09375
- w_down: bfloat16 [4, 3200, 4096], P('pool', 'tp'), may hold values from -0.109375 to 0.109375
Outputs:
- mixed: bfloat16 [512, 4096], P(('parts', 'pool', 'tp')), parts along dimension 0
There are 2 independent parts, one for each index of `parts`. A program takes and returns all parts, laid end to end along the dimension named above; an argument that names none is the same for every part. Nothing has to cross between parts.
Inputs may be any that keep to these rules, and one draw needn't show every extreme that they name: `cache_len`: some request has a full cache. `draft_count`: some request has 32 draft rows. `routes`: the 2 ids of a row differ. Within the rows of one device, the routes to one expert taken in order of row and then of k get slots 0, 1, 2 and so on; those past the first 12 get -1; in every draw some expert gets all 12 slots from every device.
All inputs are finite; a program needn't handle non-finite values.
Results may differ from a plain program's by a relative error of at most 0.015.
Values may be sent and summed in bfloat16 or wider, within the bound.
A program may use at most 64 MiB of HBM per device.

v0:
```python
import functools

import jax
import jax.numpy as jnp
from jax import lax
from jax.experimental import pallas as pl
from jax.experimental.pallas import tpu as pltpu
from jax.sharding import PartitionSpec as P

HD = 128
LANES = 128
CORES = 2
MESH = pl.DeviceIdType.MESH
F32 = jnp.float32
BF16 = jnp.bfloat16


def remote(src, dst, send_sem, recv_sem, where):
    return pltpu.make_async_remote_copy(
        src_ref=src,
        dst_ref=dst,
        send_sem=send_sem,
        recv_sem=recv_sem,
        device_id=where,
        device_id_type=MESH,
    )


def kernel(
    pool_count,
    tp_count,
    chunks,
    cache_len,
    draft_count,
    routes,
    slots,
    route_weights,
    residual_hbm,
    queries_hbm,
    new_kv_hbm,
    cache_hbm,
    out_proj_hbm,
    gain_hbm,
    w_gate_hbm,
    w_up_hbm,
    w_down_hbm,
    out_ref,
    residual,
    queries,
    new_kv,
    cache,
    out_proj,
    gain,
    w_gate,
    w_up,
    w_down,
    attended,
    proj_part,
    proj_in,
    hidden,
    rows_all,
    weights_all,
    gate_acc,
    up_acc,
    act,
    part_all,
    core_in,
    pair_in,
    pair_sum,
    line_in,
    load_sem,
    ps_sem,
    pr_sem,
    wzs_sem,
    wzr_sem,
    wys_sem,
    wyr_sem,
    wc_sem,
    gzs_sem,
    gzr_sem,
    gys_sem,
    gyr_sem,
    gcs_sem,
    gcr_sem,
    szs_sem,
    szr_sem,
    sys_sem,
    syr_sem,
    scs_sem,
    scr_sem,
):
    y_count = pool_count // CORES
    pool_me = lax.axis_index("pool")
    z_me = lax.axis_index("tp")
    y_me = pool_me // CORES
    c_me = lax.rem(pool_me, CORES)
    c_other = 1 - c_me
    core_dev = {"pool": y_me * CORES + c_other}

    def z_at(step):
        return lax.rem(z_me + step, tp_count)

    def y_at(step):
        return lax.rem(y_me + step, y_count)

    def z_dev(z):
        return {"tp": z}

    def y_dev(y):
        return {"pool": y * CORES + c_me}

    rows, dim = residual.shape
    line_rows = tp_count * rows
    half_rows = y_count * line_rows
    all_rows = CORES * half_rows
    width = dim // chunks

    def cols(k):
        return pl.ds(pl.multiple_of(k * width, width), width)

    def row_ds(start, size):
        return pl.ds(pl.multiple_of(start, size), size)

    loads = [
        pltpu.make_async_copy(src, dst, load_sem.at[n])
        for n, (src, dst) in enumerate(
            [
                (queries_hbm, queries),
                (cache_hbm, cache),
                (new_kv_hbm, new_kv),
                (out_proj_hbm, out_proj),
                (residual_hbm, residual),
                (gain_hbm, gain),
                (w_gate_hbm, w_gate),
                (w_up_hbm, w_up),
                (w_down_hbm, w_down),
            ]
        )
    ]
    for load in loads:
        load.start()

    barrier = pltpu.get_barrier_semaphore()
    partners = (
        [core_dev]
        + [y_dev(y_at(s)) for s in range(1, y_count)]
        + [z_dev(z_at(s)) for s in range(1, tp_count)]
    )
    for partner in partners:
        pl.semaphore_signal(barrier, inc=1, device_id=partner, device_id_type=MESH)
    pl.semaphore_wait(barrier, len(partners))

    half_at = c_me * half_rows
    line_at = half_at + y_me * line_rows
    own_at = line_at + z_me * rows

    lane = lax.broadcasted_iota(jnp.int32, (rows, weights_all.shape[1]), 1)
    dense = jnp.zeros((rows, weights_all.shape[1]), F32)
    for k in range(routes.shape[1]):
        hit = (routes[:, k : k + 1] == lane) & (slots[:, k : k + 1] >= 0)
        dense = dense + jnp.where(hit, route_weights[:, k : k + 1].astype(F32), 0.0)
    weights_all[row_ds(own_at, rows), :] = dense.astype(BF16)

    def w_line(step, z_from):
        block = weights_all.at[row_ds(line_at + z_from * rows, rows), :]
        z_to = z_at(step)
        return block, z_to

    def w_z_send(step):
        block = weights_all.at[row_ds(own_at, rows), :]
        z_to = z_at(step)
        return remote(block, block, wzs_sem.at[z_to], wzr_sem.at[z_me], z_dev(z_to))

    def w_z_recv(step):
        z_from = z_at(step)
        block = weights_all.at[row_ds(line_at + z_from * rows, rows), :]
        return remote(block, block, wzs_sem.at[z_from], wzr_sem.at[z_from], z_dev(z_from))

    def w_y_send(step):
        block = weights_all.at[row_ds(line_at, line_rows), :]
        y_to = y_at(step)
        return remote(block, block, wys_sem.at[y_to], wyr_sem.at[y_me], y_dev(y_to))

    def w_y_recv(step):
        y_from = y_at(step)
        block = weights_all.at[row_ds(half_at + y_from * line_rows, line_rows), :]
        return remote(block, block, wys_sem.at[y_from], wyr_sem.at[y_from], y_dev(y_from))

    def w_c_send():
        block = weights_all.at[row_ds(half_at, half_rows), :]
        return remote(block, block, wc_sem.at[0], wc_sem.at[1], core_dev)

    def w_c_recv():
        block = weights_all.at[row_ds(c_other * half_rows, half_rows), :]
        return remote(block, block, wc_sem.at[0], wc_sem.at[1], core_dev)

    for s in range(1, tp_count):
        w_z_send(s).start()

    for load in loads[:3]:
        load.wait()
    requests, cache_size = cache.shape[1], cache.shape[2]
    kv_here = cache.shape[3] // HD
    draft = queries.shape[0] // requests
    group = queries.shape[1] // HD // kv_here
    scale = HD ** (-0.5)
    nt = (((1,), (1,)), ((), ()))
    for r in range(requests):
        span = slice(r * draft, (r + 1) * draft)
        for h in range(kv_here):
            kv_cols = slice(h * HD, (h + 1) * HD)
            q = jnp.concatenate(
                [
                    queries[span, (h * group + g) * HD : (h * group + g + 1) * HD]
                    for g in range(group)
                ],
                axis=0,
            )
            old = lax.dot_general(q, cache[0, r, :, kv_cols], nt, preferred_element_type=F32) * scale
            new = lax.dot_general(q, new_kv[0, span, kv_cols], nt, preferred_element_type=F32) * scale
            old_at = lax.broadcasted_iota(jnp.int32, old.shape, 1)
            new_at = lax.broadcasted_iota(jnp.int32, new.shape, 1)
            new_row = lax.rem(lax.broadcasted_iota(jnp.int32, new.shape, 0), draft)
            see_old = old_at < cache_len[r]
            see_new = (new_at <= new_row) & (new_at < draft_count[r])
            top = jnp.maximum(
                jnp.max(jnp.where(see_old, old, -1e30), axis=1, keepdims=True),
                jnp.max(jnp.where(see_new, new, -1e30), axis=1, keepdims=True),
            )
            p_old = jnp.where(see_old, jnp.exp(old - top), 0.0)
            p_new = jnp.where(see_new, jnp.exp(new - top), 0.0)
            total = jnp.sum(p_old, axis=1, keepdims=True) + jnp.sum(p_new, axis=1, keepdims=True)
            a_old = (p_old / total).astype(BF16)
            a_new = (p_new / total).astype(BF16)
            res = jnp.dot(a_old, cache[1, r, :, kv_cols], preferred_element_type=F32)
            res = res + jnp.dot(a_new, new_kv[1, span, kv_cols], preferred_element_type=F32)
            for g in range(group):
                attended[span, (h * group + g) * HD : (h * group + g + 1) * HD] = res[
                    g * draft : (g + 1) * draft
                ].astype(BF16)

    def proj_send(k, step):
        z_to = z_at(step)
        return remote(
            proj_part.at[row_ds(z_to * rows, rows), cols(k)],
            proj_in.at[z_me, :, cols(k)],
            ps_sem.at[k, z_to],
            pr_sem.at[k, z_me],
            z_dev(z_to),
        )

    def proj_recv(k, step):
        z_from = z_at(step)
        block = proj_in.at[z_from, :, cols(k)]
        return remote(
            proj_part.at[row_ds(z_from * rows, rows), cols(k)],
            block,
            ps_sem.at[k, z_from],
            pr_sem.at[k, z_from],
            z_dev(z_from),
        )

    loads[3].wait()

    def project(k, carry):
        proj_part[:, cols(k)] = jnp.dot(
            attended[...], out_proj[:, cols(k)], preferred_element_type=F32
        ).astype(BF16)
        for s in range(1, tp_count):
            proj_send(k, s).start()
        return carry

    lax.fori_loop(0, chunks, project, 0)

    for s in range(1, tp_count):
        w_z_recv(s).wait_recv()
    for s in range(1, y_count):
        w_y_send(s).start()
    for s in range(1, y_count):
        w_y_recv(s).wait_recv()
    w_c_send().start()

    loads[4].wait()
    loads[5].wait()

    def add_residual(k, power):
        for s in range(1, tp_count):
            proj_recv(k, s).wait_recv()
        total = proj_part[row_ds(z_me * rows, rows), cols(k)].astype(F32)
        for s in range(1, tp_count):
            total = total + proj_in[z_at(s), :, cols(k)].astype(F32)
        h = (residual[:, cols(k)].astype(F32) + total).astype(BF16)
        hidden[:, cols(k)] = h
        wide = h.astype(F32)
        return power + jnp.sum(wide * wide, axis=1, keepdims=True)

    power = lax.fori_loop(0, chunks, add_residual, jnp.zeros((rows, 1), F32))
    factor = lax.rsqrt(power / dim + 1e-05)

    def g_z_send(k, step):
        z_to = z_at(step)
        block = rows_all.at[row_ds(own_at, rows), cols(k)]
        return remote(block, block, gzs_sem.at[k, z_to], gzr_sem.at[k, z_me], z_dev(z_to))

    def g_z_recv(k, step):
        z_from = z_at(step)
        block = rows_all.at[row_ds(line_at + z_from * rows, rows), cols(k)]
        return remote(block, block, gzs_sem.at[k, z_from], gzr_sem.at[k, z_from], z_dev(z_from))

    def g_y_send(k, step):
        y_to = y_at(step)
        block = rows_all.at[row_ds(line_at, line_rows), cols(k)]
        return remote(block, block, gys_sem.at[k, y_to], gyr_sem.at[k, y_me], y_dev(y_to))

    def g_y_recv(k, step):
        y_from = y_at(step)
        block = rows_all.at[row_ds(half_at + y_from * line_rows, line_rows), cols(k)]
        return remote(block, block, gys_sem.at[k, y_from], gyr_sem.at[k, y_from], y_dev(y_from))

    def g_c_send(k):
        block = rows_all.at[row_ds(half_at, half_rows), cols(k)]
        return remote(block, block, gcs_sem.at[k], gcr_sem.at[k], core_dev)

    def g_c_recv(k):
        block = rows_all.at[row_ds(c_other * half_rows, half_rows), cols(k)]
        return remote(block, block, gcs_sem.at[k], gcr_sem.at[k], core_dev)

    def norm(k, carry):
        normed = hidden[:, cols(k)].astype(F32) * factor * gain[:, cols(k)]
        rows_all[row_ds(own_at, rows), cols(k)] = normed.astype(BF16)
        for s in range(1, tp_count):
            g_z_send(k, s).start()
        return carry

    lax.fori_loop(0, chunks, norm, 0)

    gate_acc[...] = jnp.zeros_like(gate_acc)
    up_acc[...] = jnp.zeros_like(up_acc)
    w_c_recv().wait_recv()
    loads[6].wait()
    loads[7].wait()

    def first(i, carry):
        @pl.when(i < chunks)
        def _():
            for s in range(1, tp_count):
                g_z_recv(i, s).wait_recv()
            for s in range(1, y_count):
                g_y_send(i, s).start()

        @pl.when((i >= 1) & (i < chunks + 1))
        def _():
            for s in range(1, y_count):
                g_y_recv(i - 1, s).wait_recv()
            g_c_send(i - 1).start()

        @pl.when(i >= 2)
        def _():
            k = i - 2
            g_c_recv(k).wait_recv()
            block = rows_all[:, cols(k)]
            gate_acc[...] += jnp.dot(block, w_gate[0, cols(k), :], preferred_element_type=F32)
            up_acc[...] += jnp.dot(block, w_up[0, cols(k), :], preferred_element_type=F32)

        return carry

    lax.fori_loop(0, chunks + 2, first, 0)

    gate = gate_acc[...]
    act[...] = (gate / (1.0 + jnp.exp(-gate)) * up_acc[...]).astype(BF16)
    expert_lane = lax.broadcasted_iota(jnp.int32, weights_all.shape, 1) == pool_me
    combine = jnp.sum(
        jnp.where(expert_lane, weights_all[...].astype(F32), 0.0), axis=1, keepdims=True
    )

    def s_c_send(k):
        return remote(
            part_all.at[row_ds(c_other * half_rows, half_rows), cols(k)],
            core_in.at[:, cols(k)],
            scs_sem.at[k],
            scr_sem.at[k],
            core_dev,
        )

    def s_y_send(k, step):
        y_to = y_at(step)
        return remote(
            core_in.at[row_ds(y_to * line_rows, line_rows), cols(k)],
            pair_in.at[y_me, :, cols(k)],
            sys_sem.at[k, y_to],
            syr_sem.at[k, y_me],
            y_dev(y_to),
        )

    def s_y_recv(k, step):
        y_from = y_at(step)
        return remote(
            core_in.at[row_ds(y_from * line_rows, line_rows), cols(k)],
            pair_in.at[y_from, :, cols(k)],
            sys_sem.at[k, y_from],
            syr_sem.at[k, y_from],
            y_dev(y_from),
        )

    def s_z_send(k, step):
        z_to = z_at(step)
        return remote(
            pair_sum.at[row_ds(z_to * rows, rows), cols(k)],
            line_in.at[z_me, :, cols(k)],
            szs_sem.at[k, z_to],
            szr_sem.at[k, z_me],
            z_dev(z_to),
        )

    def s_z_recv(k, step):
        z_from = z_at(step)
        return remote(
            pair_sum.at[row_ds(z_from * rows, rows), cols(k)],
            line_in.at[z_from, :, cols(k)],
            szs_sem.at[k, z_from],
            szr_sem.at[k, z_from],
            z_dev(z_from),
        )

    loads[8].wait()

    def second(i, carry):
        @pl.when(i < chunks)
        def _():
            part = jnp.dot(act[...], w_down[0, :, cols(i)], preferred_element_type=F32)
            part_all[:, cols(i)] = (part * combine).astype(BF16)
            s_c_send(i).start()

        @pl.when((i >= 1) & (i < chunks + 1))
        def _():
            k = i - 1
            s_c_send(k).wait_recv()
            core_in[:, cols(k)] = (
                core_in[:, cols(k)].astype(F32)
                + part_all[row_ds(half_at, half_rows), cols(k)].astype(F32)
            ).astype(BF16)
            for s in range(1, y_count):
                s_y_send(k, s).start()

        @pl.when((i >= 2) & (i < chunks + 2))
        def _():
            k = i - 2
            total = core_in[row_ds(y_me * line_rows, line_rows), cols(k)].astype(F32)
            for s in range(1, y_count):
                s_y_recv(k, s).wait_recv()
                total = total + pair_in[y_at(s), :, cols(k)].astype(F32)
            pair_sum[:, cols(k)] = total.astype(BF16)
            for s in range(1, tp_count):
                s_z_send(k, s).start()

        @pl.when(i >= 3)
        def _():
            k = i - 3
            total = pair_sum[row_ds(z_me * rows, rows), cols(k)].astype(F32)
            for s in range(1, tp_count):
                s_z_recv(k, s).wait_recv()
                total = total + line_in[z_at(s), :, cols(k)].astype(F32)
            out_ref[:, cols(k)] = (hidden[:, cols(k)].astype(F32) + total).astype(BF16)

        return carry

    lax.fori_loop(0, chunks + 3, second, 0)

    for s in range(1, tp_count):
        w_z_send(s).wait_send()
    for s in range(1, y_count):
        w_y_send(s).wait_send()
    w_c_send().wait_send()

    def drain(k, carry):
        for s in range(1, tp_count):
            proj_send(k, s).wait_send()
            g_z_send(k, s).wait_send()
            s_z_send(k, s).wait_send()
        for s in range(1, y_count):
            g_y_send(k, s).wait_send()
            s_y_send(k, s).wait_send()
        g_c_send(k).wait_send()
        s_c_send(k).wait_send()
        return carry

    lax.fori_loop(0, chunks, drain, 0)


def local(
    pool_count,
    tp_count,
    residual,
    queries,
    new_kv,
    cache,
    cache_len,
    draft_count,
    out_proj,
    norm_gain,
    routes,
    slots,
    route_weights,
    w_gate,
    w_up,
    w_down,
):
    rows, dim = residual.shape
    y_count = pool_count // CORES
    line_rows = tp_count * rows
    half_rows = y_count * line_rows
    all_rows = CORES * half_rows
    hidden_units = w_gate.shape[2]
    weight_lanes = pl.cdiv(pool_count, LANES) * LANES
    chunks = 4
    gain = norm_gain.reshape(1, dim)
    dma = pltpu.SemaphoreType.DMA
    loaded = (residual, queries, new_kv, cache, out_proj, gain, w_gate, w_up, w_down)
    smem = pl.BlockSpec(memory_space=pltpu.SMEM)
    vmem = pl.BlockSpec(memory_space=pltpu.VMEM)
    return pl.pallas_call(
        functools.partial(kernel, pool_count, tp_count, chunks),
        out_shape=jax.ShapeDtypeStruct((rows, dim), BF16),
        in_specs=[smem] * 2 + [vmem] * 3 + [pl.BlockSpec(memory_space=pl.ANY)] * len(loaded),
        out_specs=vmem,
        scratch_shapes=[pltpu.VMEM(a.shape, a.dtype) for a in loaded]
        + [
            pltpu.VMEM((queries.shape[0], queries.shape[1]), BF16),
            pltpu.VMEM((line_rows, dim), BF16),
            pltpu.VMEM((tp_count, rows, dim), BF16),
            pltpu.VMEM((rows, dim), BF16),
            pltpu.VMEM((all_rows, dim), BF16),
            pltpu.VMEM((all_rows, weight_lanes), BF16),
            pltpu.VMEM((all_rows, hidden_units), F32),
            pltpu.VMEM((all_rows, hidden_units), F32),
            pltpu.VMEM((all_rows, hidden_units), BF16),
            pltpu.VMEM((all_rows, dim), BF16),
            pltpu.VMEM((half_rows, dim), BF16),
            pltpu.VMEM((y_count, line_rows, dim), BF16),
            pltpu.VMEM((line_rows, dim), BF16),
            pltpu.VMEM((tp_count, rows, dim), BF16),
            dma((len(loaded),)),
            dma((chunks, tp_count)),
            dma((chunks, tp_count)),
            dma((tp_count,)),
            dma((tp_count,)),
            dma((y_count,)),
            dma((y_count,)),
            dma((2,)),
            dma((chunks, tp_count)),
            dma((chunks, tp_count)),
            dma((chunks, y_count)),
            dma((chunks, y_count)),
            dma((chunks,)),
            dma((chunks,)),
            dma((chunks, tp_count)),
            dma((chunks, tp_count)),
            dma((chunks, y_count)),
            dma((chunks, y_count)),
            dma((chunks,)),
            dma((chunks,)),
        ],
        compiler_params=pltpu.CompilerParams(
            collective_id=0, has_side_effects=True, vmem_limit_bytes=60 * 1024 * 1024
        ),
    )(cache_len, draft_count, routes, slots, route_weights, *loaded)


def solution(mesh):
    in_specs = (
        P(("parts", "pool", "tp"), None),
        P(("parts", "pool"), "tp"),
        P(None, ("parts", "pool"), "tp"),
        P(None, ("parts", "pool"), None, "tp"),
        P(("parts", "pool")),
        P(("parts", "pool")),
        P("tp", None),
        P(),
        P(("parts", "pool", "tp"), None),
        P(("parts", "pool", "tp"), None),
        P(("parts", "pool", "tp"), None),
        P("pool", None, "tp"),
        P("pool", None, "tp"),
        P("pool", "tp", None),
    )
    out_specs = P(("parts", "pool", "tp"), None)
    body = functools.partial(local, mesh.shape["pool"], mesh.shape["tp"])
    return jax.shard_map(body, mesh=mesh, in_specs=in_specs, out_specs=out_specs, check_vma=False)
```

profile of v0, /device:TPU:0, one launch (start us, length us, event | category | flops | bytes accessed | tf_op | source)
XLA Modules:
  0.0 92.0 jit_solution(4539424188647720189)
XLA Ops:
  0.0 1.3 %copy.17.route_weights = bf16[16,2]{1,0:T(8,128)(2,1)} copy(bf16[16,2]{0,1:T(2,128)(2,1)} %param.24) | data formatting | bytes 128 | tf_op args[10]
  1.3 1.4 %copy.15.routes = s32[16,2]{1,0:T(8,128)} copy(s32[16,2]{0,1:T(2,128)} %param.22) | data formatting | bytes 256 | tf_op args[8]
  2.7 1.4 %copy.16.slots = s32[16,2]{1,0:T(8,128)} copy(s32[16,2]{0,1:T(2,128)} %param.23) | data formatting | bytes 256 | tf_op args[9]
  4.0 10.5 %copy.18.w_gate_hbm = bf16[1,4096,800]{2,1,0:T(8,128)(2,1)} copy(bf16[1,4096,800]{1,2,0:T(8,128)(2,1)} %param.25) | data formatting | bytes 13107200 | tf_op args[11]
  14.6 10.6 %copy.19.w_up_hbm = bf16[1,4096,800]{2,1,0:T(8,128)(2,1)} copy(bf16[1,4096,800]{1,2,0:T(8,128)(2,1)} %param.26) | data formatting | bytes 13107200 | tf_op args[12]
  25.1 65.3 %shard_map.136 = bf16[16,4096]{1,0:T(8,128)(2,1)} custom-call(s32[2]{0:T(128)} %cache_len.1, s32[2]{0:T(128)} %draft_count.1, s32[16,2]{1,0:T(8,128)} %copy.15.routes, s32[16,2]{1,0:T(8,128)} %copy.16.slots, bf16[16,2]{1,0:T(8,128)(2,1)} %copy.17.route_weights, bf16[16,4096]{1,0:T(8,128)(2,1)} %residual_hbm.1, bf16[64,512]{1,0:T(8,128)(2,1)} %queries_hbm.1, ...), custom_call_target="tpu_custom_call" | custom-call | tf_op jit(solution)/shard_map/pallas_call | solution.py:521
  90.4 1.6 %copy.21 = bf16[16,4096]{1,0:T(8,128)(2,1)} copy(bf16[16,4096]{1,0:T(8,128)(2,1)} %shard_map.136) | data formatting | bytes 262144
where the time goes:
time: 92.7 us; the launch traced here: 92 us
  Pallas kernels  65.3 us (70%)
  local copies, waits for them, and re-layouts  26.7 us (29%)
    pallas_call x1, Pallas kernels, local(): pl.pallas_call(functools.partial(kernel, pool_count, tp_count, chunks), o...  65.3 us
    unnamed x6, local copies, waits for them, and re-layouts  26.7 us

commit v1 on v0

--- a/solution.py
+++ b/solution.py
@@ -154,17 +154,19 @@
     line_at = half_at + y_me * line_rows
     own_at = line_at + z_me * rows
 
-    lane = lax.broadcasted_iota(jnp.int32, (rows, weights_all.shape[1]), 1)
-    dense = jnp.zeros((rows, weights_all.shape[1]), F32)
-    for k in range(routes.shape[1]):
-        hit = (routes[:, k : k + 1] == lane) & (slots[:, k : k + 1] >= 0)
-        dense = dense + jnp.where(hit, route_weights[:, k : k + 1].astype(F32), 0.0)
-    weights_all[row_ds(own_at, rows), :] = dense.astype(BF16)
-
-    def w_line(step, z_from):
-        block = weights_all.at[row_ds(line_at + z_from * rows, rows), :]
-        z_to = z_at(step)
-        return block, z_to
+    lanes = weights_all.shape[1]
+    expert = lax.broadcasted_iota(jnp.int32, (lanes, rows), 0)
+    dense = jnp.zeros((lanes, rows), F32)
+    for k in range(routes.shape[0]):
+        hit = (routes[k : k + 1, :] == expert) & (slots[k : k + 1, :] >= 0)
+        dense = dense + jnp.where(hit, route_weights[k : k + 1, :].astype(F32), 0.0)
+    same = lax.broadcasted_iota(jnp.int32, (lanes, lanes), 0) == lax.broadcasted_iota(
+        jnp.int32, (lanes, lanes), 1
+    )
+    tn = (((0,), (0,)), ((), ()))
+    weights_all[row_ds(own_at, rows), :] = lax.dot_general(
+        dense.astype(BF16), same.astype(F32).astype(BF16), tn, preferred_element_type=F32
+    ).astype(BF16)
 
     def w_z_send(step):
         block = weights_all.at[row_ds(own_at, rows), :]
@@ -359,8 +361,12 @@
             k = i - 2
             g_c_recv(k).wait_recv()
             block = rows_all[:, cols(k)]
-            gate_acc[...] += jnp.dot(block, w_gate[0, cols(k), :], preferred_element_type=F32)
-            up_acc[...] += jnp.dot(block, w_up[0, cols(k), :], preferred_element_type=F32)
+            gate_acc[...] += lax.dot_general(
+                block, w_gate[0, :, cols(k)], nt, preferred_element_type=F32
+            )
+            up_acc[...] += lax.dot_general(
+                block, w_up[0, :, cols(k)], nt, preferred_element_type=F32
+            )
 
         return carry
 
@@ -510,10 +516,12 @@
     line_rows = tp_count * rows
     half_rows = y_count * line_rows
     all_rows = CORES * half_rows
-    hidden_units = w_gate.shape[2]
+    hidden_units = w_down.shape[1]
     weight_lanes = pl.cdiv(pool_count, LANES) * LANES
     chunks = 4
     gain = norm_gain.reshape(1, dim)
+    w_gate, w_up = jnp.swapaxes(w_gate, 1, 2), jnp.swapaxes(w_up, 1, 2)
+    routes, slots, route_weights = routes.T, slots.T, route_weights.T
     dma = pltpu.SemaphoreType.DMA
     loaded = (residual, queries, new_kv, cache, out_proj, gain, w_gate, w_up, w_down)
     smem = pl.BlockSpec(memory_space=pltpu.SMEM)

time: 92.7 us -> 67.4 us (0.73)
  local copies, waits for them, and re-layouts: 26.7 us -> 1.57 us
    unnamed x6 -> x1, local copies, waits for them, and re-layouts: 26.7 us -> 1.57 us
where the time goes in v1:
time: 67.4 us; the launch traced here: 67.3 us
  Pallas kernels  65.7 us (97%)
  local copies, waits for them, and re-layouts  1.57 us (2%)
    pallas_call x1, Pallas kernels, local(): pl.pallas_call(functools.partial(kernel, pool_count, tp_count, chunks), o...  65.7 us
    unnamed x1, local copies, waits for them, and re-layouts  1.57 us

profile of v1, /device:TPU:0, one launch (start us, length us, event | category | flops | bytes accessed | tf_op | source)
XLA Modules:
  0.0 67.3 jit_solution(1703885818959979219)
XLA Ops:
  0.0 65.7 %shard_map.136 = bf16[16,4096]{1,0:T(8,128)(2,1)} custom-call(s32[2]{0:T(128)} %cache_len.1, s32[2]{0:T(128)} %draft_count.1, s32[2,16]{1,0:T(2,128)} %bitcast.9, s32[2,16]{1,0:T(2,128)} %bitcast.10, bf16[2,16]{1,0:T(2,128)(2,1)} %bitcast.11, bf16[16,4096]{1,0:T(8,128)(2,1)} %residual_hbm.1, bf16[64,512]{1,0:T(8,128)(2,1)} %queries_hbm.1, ...), custom_call_target="tpu_custom_call" | custom-call | tf_op jit(solution)/shard_map/pallas_call | solution.py:529
  65.7 1.6 %copy.16 = bf16[16,4096]{1,0:T(8,128)(2,1)} copy(bf16[16,4096]{1,0:T(8,128)(2,1)} %shard_map.136) | data formatting | bytes 262144

commit v2 on v1

--- a/solution.py
+++ b/solution.py
@@ -30,6 +30,7 @@
     pool_count,
     tp_count,
     chunks,
+    lag,
     cache_len,
     draft_count,
     routes,
@@ -60,6 +61,7 @@
     hidden,
     rows_all,
     weights_all,
+    power,
     gate_acc,
     up_acc,
     act,
@@ -137,7 +139,7 @@
             ]
         )
     ]
-    for load in loads:
+    for load in loads[:6]:
         load.start()
 
     barrier = pltpu.get_barrier_semaphore()
@@ -148,25 +150,9 @@
     )
     for partner in partners:
         pl.semaphore_signal(barrier, inc=1, device_id=partner, device_id_type=MESH)
-    pl.semaphore_wait(barrier, len(partners))
-
     half_at = c_me * half_rows
     line_at = half_at + y_me * line_rows
     own_at = line_at + z_me * rows
-
-    lanes = weights_all.shape[1]
-    expert = lax.broadcasted_iota(jnp.int32, (lanes, rows), 0)
-    dense = jnp.zeros((lanes, rows), F32)
-    for k in range(routes.shape[0]):
-        hit = (routes[k : k + 1, :] == expert) & (slots[k : k + 1, :] >= 0)
-        dense = dense + jnp.where(hit, route_weights[k : k + 1, :].astype(F32), 0.0)
-    same = lax.broadcasted_iota(jnp.int32, (lanes, lanes), 0) == lax.broadcasted_iota(
-        jnp.int32, (lanes, lanes), 1
-    )
-    tn = (((0,), (0,)), ((), ()))
-    weights_all[row_ds(own_at, rows), :] = lax.dot_general(
-        dense.astype(BF16), same.astype(F32).astype(BF16), tn, preferred_element_type=F32
-    ).astype(BF16)
 
     def w_z_send(step):
         block = weights_all.at[row_ds(own_at, rows), :]
@@ -195,9 +181,6 @@
     def w_c_recv():
         block = weights_all.at[row_ds(c_other * half_rows, half_rows), :]
         return remote(block, block, wc_sem.at[0], wc_sem.at[1], core_dev)
-
-    for s in range(1, tp_count):
-        w_z_send(s).start()
 
     for load in loads[:3]:
         load.wait()
@@ -244,8 +227,8 @@
     def proj_send(k, step):
         z_to = z_at(step)
         return remote(
-            proj_part.at[row_ds(z_to * rows, rows), cols(k)],
-            proj_in.at[z_me, :, cols(k)],
+            proj_part.at[k, row_ds(z_to * rows, rows), :],
+            proj_in.at[k, z_me],
             ps_sem.at[k, z_to],
             pr_sem.at[k, z_me],
             z_dev(z_to),
@@ -253,19 +236,37 @@
 
     def proj_recv(k, step):
         z_from = z_at(step)
-        block = proj_in.at[z_from, :, cols(k)]
+        block = proj_in.at[k, z_from]
         return remote(
-            proj_part.at[row_ds(z_from * rows, rows), cols(k)],
+            proj_part.at[k, row_ds(z_from * rows, rows), :],
             block,
             ps_sem.at[k, z_from],
             pr_sem.at[k, z_from],
             z_dev(z_from),
         )
 
+    lanes = weights_all.shape[1]
+    expert = lax.broadcasted_iota(jnp.int32, (lanes, rows), 0)
+    dense = jnp.zeros((lanes, rows), F32)
+    for k in range(routes.shape[0]):
+        hit = (routes[k : k + 1, :] == expert) & (slots[k : k + 1, :] >= 0)
+        dense = dense + jnp.where(hit, route_weights[k : k + 1, :].astype(F32), 0.0)
+    same = lax.broadcasted_iota(jnp.int32, (lanes, lanes), 0) == lax.broadcasted_iota(
+        jnp.int32, (lanes, lanes), 1
+    )
+    tn = (((0,), (0,)), ((), ()))
+    weights_all[row_ds(own_at, rows), :] = lax.dot_general(
+        dense.astype(BF16), same.astype(F32).astype(BF16), tn, preferred_element_type=F32
+    )
+
     loads[3].wait()
+    for load in loads[6:]:
+        load.start()
+
+    pl.semaphore_wait(barrier, len(partners))
 
     def project(k, carry):
-        proj_part[:, cols(k)] = jnp.dot(
+        proj_part[k] = jnp.dot(
             attended[...], out_proj[:, cols(k)], preferred_element_type=F32
         ).astype(BF16)
         for s in range(1, tp_count):
@@ -274,71 +275,40 @@
 
     lax.fori_loop(0, chunks, project, 0)
 
-    for s in range(1, tp_count):
-        w_z_recv(s).wait_recv()
-    for s in range(1, y_count):
-        w_y_send(s).start()
-    for s in range(1, y_count):
-        w_y_recv(s).wait_recv()
-    w_c_send().start()
-
     loads[4].wait()
     loads[5].wait()
 
-    def add_residual(k, power):
-        for s in range(1, tp_count):
-            proj_recv(k, s).wait_recv()
-        total = proj_part[row_ds(z_me * rows, rows), cols(k)].astype(F32)
-        for s in range(1, tp_count):
-            total = total + proj_in[z_at(s), :, cols(k)].astype(F32)
-        h = (residual[:, cols(k)].astype(F32) + total).astype(BF16)
-        hidden[:, cols(k)] = h
-        wide = h.astype(F32)
-        return power + jnp.sum(wide * wide, axis=1, keepdims=True)
-
-    power = lax.fori_loop(0, chunks, add_residual, jnp.zeros((rows, 1), F32))
-    factor = lax.rsqrt(power / dim + 1e-05)
-
     def g_z_send(k, step):
         z_to = z_at(step)
-        block = rows_all.at[row_ds(own_at, rows), cols(k)]
+        block = rows_all.at[k, row_ds(own_at, rows), :]
         return remote(block, block, gzs_sem.at[k, z_to], gzr_sem.at[k, z_me], z_dev(z_to))
 
     def g_z_recv(k, step):
         z_from = z_at(step)
-        block = rows_all.at[row_ds(line_at + z_from * rows, rows), cols(k)]
+        block = rows_all.at[k, row_ds(line_at + z_from * rows, rows), :]
         return remote(block, block, gzs_sem.at[k, z_from], gzr_sem.at[k, z_from], z_dev(z_from))
 
     def g_y_send(k, step):
         y_to = y_at(step)
-        block = rows_all.at[row_ds(line_at, line_rows), cols(k)]
+        block = rows_all.at[k, row_ds(line_at, line_rows), :]
         return remote(block, block, gys_sem.at[k, y_to], gyr_sem.at[k, y_me], y_dev(y_to))
 
     def g_y_recv(k, step):
         y_from = y_at(step)
-        block = rows_all.at[row_ds(half_at + y_from * line_rows, line_rows), cols(k)]
+        block = rows_all.at[k, row_ds(half_at + y_from * line_rows, line_rows), :]
         return remote(block, block, gys_sem.at[k, y_from], gyr_sem.at[k, y_from], y_dev(y_from))
 
     def g_c_send(k):
-        block = rows_all.at[row_ds(half_at, half_rows), cols(k)]
+        block = rows_all.at[k, row_ds(half_at, half_rows), :]
         return remote(block, block, gcs_sem.at[k], gcr_sem.at[k], core_dev)
 
     def g_c_recv(k):
-        block = rows_all.at[row_ds(c_other * half_rows, half_rows), cols(k)]
+        block = rows_all.at[k, row_ds(c_other * half_rows, half_rows), :]
         return remote(block, block, gcs_sem.at[k], gcr_sem.at[k], core_dev)
-
-    def norm(k, carry):
-        normed = hidden[:, cols(k)].astype(F32) * factor * gain[:, cols(k)]
-        rows_all[row_ds(own_at, rows), cols(k)] = normed.astype(BF16)
-        for s in range(1, tp_count):
-            g_z_send(k, s).start()
-        return carry
-
-    lax.fori_loop(0, chunks, norm, 0)
 
     gate_acc[...] = jnp.zeros_like(gate_acc)
     up_acc[...] = jnp.zeros_like(up_acc)
-    w_c_recv().wait_recv()
+    power[...] = jnp.zeros_like(power)
     loads[6].wait()
     loads[7].wait()
 
@@ -346,21 +316,60 @@
         @pl.when(i < chunks)
         def _():
             for s in range(1, tp_count):
-                g_z_recv(i, s).wait_recv()
+                proj_recv(i, s).wait_recv()
+            total = proj_part[i, row_ds(z_me * rows, rows), :].astype(F32)
+            for s in range(1, tp_count):
+                total = total + proj_in[i, z_at(s)].astype(F32)
+            h = (residual[:, cols(i)].astype(F32) + total).astype(BF16)
+            hidden[:, cols(i)] = h
+            wide = h.astype(F32)
+            rows_all[i, row_ds(own_at, rows), :] = (wide * gain[:, cols(i)]).astype(BF16)
+            for s in range(1, tp_count):
+                g_z_send(i, s).start()
+            power[...] += jnp.sum(wide * wide, axis=1, keepdims=True)
+
+        @pl.when(i == chunks)
+        def _():
+            factor = lax.rsqrt(power[...] / dim + 1e-05)
+            own = weights_all[row_ds(own_at, rows), :]
+            at = lax.broadcasted_iota(jnp.int32, own.shape, 1)
+            weights_all[row_ds(own_at, rows), :] = jnp.where(at == pool_count, factor, own)
+            for s in range(1, tp_count):
+                w_z_send(s).start()
+
+        @pl.when((i >= lag) & (i < chunks + lag))
+        def _():
+            k = i - lag
+            for s in range(1, tp_count):
+                g_z_recv(k, s).wait_recv()
             for s in range(1, y_count):
-                g_y_send(i, s).start()
-
-        @pl.when((i >= 1) & (i < chunks + 1))
-        def _():
+                g_y_send(k, s).start()
+
+        @pl.when(i == chunks + lag)
+        def _():
+            for s in range(1, tp_count):
+                w_z_recv(s).wait_recv()
             for s in range(1, y_count):
-                g_y_recv(i - 1, s).wait_recv()
-            g_c_send(i - 1).start()
-
-        @pl.when(i >= 2)
-        def _():
-            k = i - 2
+                w_y_send(s).start()
+
+        @pl.when((i >= 2 * lag) & (i < chunks + 2 * lag))
+        def _():
+            k = i - 2 * lag
+            for s in range(1, y_count):
+                g_y_recv(k, s).wait_recv()
+            g_c_send(k).start()
+
+        @pl.when(i == chunks + 2 * lag)
+        def _():
+            for s in range(1, y_count):
+                w_y_recv(s).wait_recv()
+            w_c_send().start()
+
+        @pl.when(i >= 3 * lag)
+        def _():
+            k = i - 3 * lag
             g_c_recv(k).wait_recv()
-            block = rows_all[:, cols(k)]
+            block = rows_all[k]
             gate_acc[...] += lax.dot_general(
                 block, w_gate[0, :, cols(k)], nt, preferred_element_type=F32
             )
@@ -370,19 +379,22 @@
 
         return carry
 
-    lax.fori_loop(0, chunks + 2, first, 0)
-
-    gate = gate_acc[...]
-    act[...] = (gate / (1.0 + jnp.exp(-gate)) * up_acc[...]).astype(BF16)
-    expert_lane = lax.broadcasted_iota(jnp.int32, weights_all.shape, 1) == pool_me
-    combine = jnp.sum(
-        jnp.where(expert_lane, weights_all[...].astype(F32), 0.0), axis=1, keepdims=True
-    )
+    lax.fori_loop(0, chunks + 3 * lag, first, 0)
+    w_c_recv().wait_recv()
+
+    def column(at):
+        lane = lax.broadcasted_iota(jnp.int32, weights_all.shape, 1)
+        return jnp.sum(jnp.where(lane == at, weights_all[...], 0.0), axis=1, keepdims=True)
+
+    factor_all = column(pool_count)
+    combine = column(pool_me)
+    gate = gate_acc[...] * factor_all
+    act[...] = (gate / (1.0 + jnp.exp(-gate)) * (up_acc[...] * factor_all)).astype(BF16)
 
     def s_c_send(k):
         return remote(
-            part_all.at[row_ds(c_other * half_rows, half_rows), cols(k)],
-            core_in.at[:, cols(k)],
+            part_all.at[k, row_ds(c_other * half_rows, half_rows), :],
+            core_in.at[k],
             scs_sem.at[k],
             scr_sem.at[k],
             core_dev,
@@ -391,8 +403,8 @@
     def s_y_send(k, step):
         y_to = y_at(step)
         return remote(
-            core_in.at[row_ds(y_to * line_rows, line_rows), cols(k)],
-            pair_in.at[y_me, :, cols(k)],
+            core_in.at[k, row_ds(y_to * line_rows, line_rows), :],
+            pair_in.at[k, y_me],
             sys_sem.at[k, y_to],
             syr_sem.at[k, y_me],
             y_dev(y_to),
@@ -401,8 +413,8 @@
     def s_y_recv(k, step):
         y_from = y_at(step)
         return remote(
-            core_in.at[row_ds(y_from * line_rows, line_rows), cols(k)],
-            pair_in.at[y_from, :, cols(k)],
+            core_in.at[k, row_ds(y_from * line_rows, line_rows), :],
+            pair_in.at[k, y_from],
             sys_sem.at[k, y_from],
             syr_sem.at[k, y_from],
             y_dev(y_from),
@@ -411,8 +423,8 @@
     def s_z_send(k, step):
         z_to = z_at(step)
         return remote(
-            pair_sum.at[row_ds(z_to * rows, rows), cols(k)],
-            line_in.at[z_me, :, cols(k)],
+            pair_sum.at[k, row_ds(z_to * rows, rows), :],
+            line_in.at[k, z_me],
             szs_sem.at[k, z_to],
             szr_sem.at[k, z_me],
             z_dev(z_to),
@@ -421,8 +433,8 @@
     def s_z_recv(k, step):
         z_from = z_at(step)
         return remote(
-            pair_sum.at[row_ds(z_from * rows, rows), cols(k)],
-            line_in.at[z_from, :, cols(k)],
+            pair_sum.at[k, row_ds(z_from * rows, rows), :],
+            line_in.at[k, z_from],
             szs_sem.at[k, z_from],
             szr_sem.at[k, z_from],
             z_dev(z_from),
@@ -434,43 +446,43 @@
         @pl.when(i < chunks)
         def _():
             part = jnp.dot(act[...], w_down[0, :, cols(i)], preferred_element_type=F32)
-            part_all[:, cols(i)] = (part * combine).astype(BF16)
+            part_all[i] = (part * combine).astype(BF16)
             s_c_send(i).start()
 
-        @pl.when((i >= 1) & (i < chunks + 1))
-        def _():
-            k = i - 1
+        @pl.when((i >= lag) & (i < chunks + lag))
+        def _():
+            k = i - lag
             s_c_send(k).wait_recv()
-            core_in[:, cols(k)] = (
-                core_in[:, cols(k)].astype(F32)
-                + part_all[row_ds(half_at, half_rows), cols(k)].astype(F32)
+            core_in[k] = (
+                core_in[k].astype(F32)
+                + part_all[k, row_ds(half_at, half_rows), :].astype(F32)
             ).astype(BF16)
             for s in range(1, y_count):
                 s_y_send(k, s).start()
 
-        @pl.when((i >= 2) & (i < chunks + 2))
-        def _():
-            k = i - 2
-            total = core_in[row_ds(y_me * line_rows, line_rows), cols(k)].astype(F32)
+        @pl.when((i >= 2 * lag) & (i < chunks + 2 * lag))
+        def _():
+            k = i - 2 * lag
+            total = core_in[k, row_ds(y_me * line_rows, line_rows), :].astype(F32)
             for s in range(1, y_count):
                 s_y_recv(k, s).wait_recv()
-                total = total + pair_in[y_at(s), :, cols(k)].astype(F32)
-            pair_sum[:, cols(k)] = total.astype(BF16)
+                total = total + pair_in[k, y_at(s)].astype(F32)
+            pair_sum[k] = total.astype(BF16)
             for s in range(1, tp_count):
                 s_z_send(k, s).start()
 
-        @pl.when(i >= 3)
-        def _():
-            k = i - 3
-            total = pair_sum[row_ds(z_me * rows, rows), cols(k)].astype(F32)
+        @pl.when(i >= 3 * lag)
+        def _():
+            k = i - 3 * lag
+            total = pair_sum[k, row_ds(z_me * rows, rows), :].astype(F32)
             for s in range(1, tp_count):
                 s_z_recv(k, s).wait_recv()
-                total = total + line_in[z_at(s), :, cols(k)].astype(F32)
+                total = total + line_in[k, z_at(s)].astype(F32)
             out_ref[:, cols(k)] = (hidden[:, cols(k)].astype(F32) + total).astype(BF16)
 
         return carry
 
-    lax.fori_loop(0, chunks + 3, second, 0)
+    lax.fori_loop(0, chunks + 3 * lag, second, 0)
 
     for s in range(1, tp_count):
         w_z_send(s).wait_send()
@@ -517,8 +529,9 @@
     half_rows = y_count * line_rows
     all_rows = CORES * half_rows
     hidden_units = w_down.shape[1]
-    weight_lanes = pl.cdiv(pool_count, LANES) * LANES
-    chunks = 4
+    weight_lanes = pl.cdiv(pool_count + 1, LANES) * LANES
+    chunks, lag = 8, 3
+    width = dim // chunks
     gain = norm_gain.reshape(1, dim)
     w_gate, w_up = jnp.swapaxes(w_gate, 1, 2), jnp.swapaxes(w_up, 1, 2)
     routes, slots, route_weights = routes.T, slots.T, route_weights.T
@@ -527,26 +540,27 @@
     smem = pl.BlockSpec(memory_space=pltpu.SMEM)
     vmem = pl.BlockSpec(memory_space=pltpu.VMEM)
     return pl.pallas_call(
-        functools.partial(kernel, pool_count, tp_count, chunks),
+        functools.partial(kernel, pool_count, tp_count, chunks, lag),
         out_shape=jax.ShapeDtypeStruct((rows, dim), BF16),
         in_specs=[smem] * 2 + [vmem] * 3 + [pl.BlockSpec(memory_space=pl.ANY)] * len(loaded),
         out_specs=vmem,
         scratch_shapes=[pltpu.VMEM(a.shape, a.dtype) for a in loaded]
         + [
             pltpu.VMEM((queries.shape[0], queries.shape[1]), BF16),
-            pltpu.VMEM((line_rows, dim), BF16),
-            pltpu.VMEM((tp_count, rows, dim), BF16),
+            pltpu.VMEM((chunks, line_rows, width), BF16),
+            pltpu.VMEM((chunks, tp_count, rows, width), BF16),
             pltpu.VMEM((rows, dim), BF16),
-            pltpu.VMEM((all_rows, dim), BF16),
-            pltpu.VMEM((all_rows, weight_lanes), BF16),
+            pltpu.VMEM((chunks, all_rows, width), BF16),
+            pltpu.VMEM((all_rows, weight_lanes), F32),
+            pltpu.VMEM((rows, weight_lanes), F32),
             pltpu.VMEM((all_rows, hidden_units), F32),
             pltpu.VMEM((all_rows, hidden_units), F32),
             pltpu.VMEM((all_rows, hidden_units), BF16),
-            pltpu.VMEM((all_rows, dim), BF16),
-            pltpu.VMEM((half_rows, dim), BF16),
-            pltpu.VMEM((y_count, line_rows, dim), BF16),
-            pltpu.VMEM((line_rows, dim), BF16),
-            pltpu.VMEM((tp_count, rows, dim), BF16),
+            pltpu.VMEM((chunks, all_rows, width), BF16),
+            pltpu.VMEM((chunks, half_rows, width), BF16),
+            pltpu.VMEM((chunks, y_count, line_rows, width), BF16),
+            pltpu.VMEM((chunks, line_rows, width), BF16),
+            pltpu.VMEM((chunks, tp_count, rows, width), BF16),
             dma((len(loaded),)),
             dma((chunks, tp_count)),
             dma((chunks, tp_count)),

time: 67.4 us -> 63.9 us (0.948)
  Pallas kernels: 65.7 us -> 62.2 us
    pallas_call x1, Pallas kernels: 65.7 us -> 62.2 us  [local(): pl.pallas_call(functools.partial(kernel, pool_count, tp_count, chunks, la...]
where the time goes in v2:
time: 63.9 us; the launch traced here: 63.8 us
  Pallas kernels  62.2 us (97%)
  local copies, waits for them, and re-layouts  1.57 us (2%)
    pallas_call x1, Pallas kernels, local(): pl.pallas_call(functools.partial(kernel, pool_count, tp_count, chunks, la...  62.2 us
    unnamed x1, local copies, waits for them, and re-layouts  1.57 us

profile of v2, /device:TPU:0, one launch (start us, length us, event | category | flops | bytes accessed | tf_op | source)
XLA Modules:
  0.0 63.8 jit_solution(5968141813618796179)
XLA Ops:
  0.0 62.2 %shard_map.136 = bf16[16,4096]{1,0:T(8,128)(2,1)} custom-call(s32[2]{0:T(128)} %cache_len.1, s32[2]{0:T(128)} %draft_count.1, s32[2,16]{1,0:T(2,128)} %bitcast.9, s32[2,16]{1,0:T(2,128)} %bitcast.10, bf16[2,16]{1,0:T(2,128)(2,1)} %bitcast.11, bf16[16,4096]{1,0:T(8,128)(2,1)} %residual_hbm.1, bf16[64,512]{1,0:T(8,128)(2,1)} %queries_hbm.1, ...), custom_call_target="tpu_custom_call" | custom-call | tf_op jit(solution)/shard_map/pallas_call | solution.py:542
  62.2 1.6 %copy.16 = bf16[16,4096]{1,0:T(8,128)(2,1)} copy(bf16[16,4096]{1,0:T(8,128)(2,1)} %shard_map.136) | data formatting | bytes 262144

commit v3 on v2

--- a/solution.py
+++ b/solution.py
@@ -309,8 +309,6 @@
     gate_acc[...] = jnp.zeros_like(gate_acc)
     up_acc[...] = jnp.zeros_like(up_acc)
     power[...] = jnp.zeros_like(power)
-    loads[6].wait()
-    loads[7].wait()
 
     def first(i, carry):
         @pl.when(i < chunks)
@@ -364,6 +362,11 @@
             for s in range(1, y_count):
                 w_y_recv(s).wait_recv()
             w_c_send().start()
+
+        @pl.when(i == 3 * lag)
+        def _():
+            loads[6].wait()
+            loads[7].wait()
 
         @pl.when(i >= 3 * lag)
         def _():

time: 63.9 us -> 63.9 us (level)
  no operation moved by 1% of the time
where the time goes in v3:
time: 63.9 us; the launch traced here: 63.8 us
  Pallas kernels  62.2 us (97%)
  local copies, waits for them, and re-layouts  1.57 us (2%)
    pallas_call x1, Pallas kernels, local(): pl.pallas_call(functools.partial(kernel, pool_count, tp_count, chunks, la...  62.2 us
    unnamed x1, local copies, waits for them, and re-layouts  1.57 us

profile of v3, /device:TPU:0, one launch (start us, length us, event | category | flops | bytes accessed | tf_op | source)
XLA Modules:
  0.0 63.8 jit_solution(4196964859933689162)
XLA Ops:
  0.0 62.2 %shard_map.136 = bf16[16,4096]{1,0:T(8,128)(2,1)} custom-call(s32[2]{0:T(128)} %cache_len.1, s32[2]{0:T(128)} %draft_count.1, s32[2,16]{1,0:T(2,128)} %bitcast.9, s32[2,16]{1,0:T(2,128)} %bitcast.10, bf16[2,16]{1,0:T(2,128)(2,1)} %bitcast.11, bf16[16,4096]{1,0:T(8,128)(2,1)} %residual_hbm.1, bf16[64,512]{1,0:T(8,128)(2,1)} %queries_hbm.1, ...), custom_call_target="tpu_custom_call" | custom-call | tf_op jit(solution)/shard_map/pallas_call | solution.py:545
  62.2 1.6 %copy.16 = bf16[16,4096]{1,0:T(8,128)(2,1)} copy(bf16[16,4096]{1,0:T(8,128)(2,1)} %shard_map.136) | data formatting | bytes 262144
